TPU v7x, 512 devices: a whole 4x8x8 slice. The times are simulated.
512 devices in a mesh: section: 4 (over x_lo, core), dp: 8 (over z), tensor: 16 (over x_hi, y).
Axes of the slice: x: 4 (x_hi: 2, x_lo: 2; x = x_hi * 2 + x_lo), y: 8, z: 8, core: 2. Of those that a mesh axis runs over, the one named last changes fastest.
Arguments:
- resid_in: bfloat16 [4, 1024, 8192], P('section', ('dp', 'tensor')), may hold values from -6 to 6
- attn_in: bfloat16 [4, 1024, 12288], P('section', 'dp', 'tensor'), may hold values from -22 to 22, as said below
- seg_fwd: int32 [4, 8, 128], P('section', 'dp'), may hold values from 0 to 7, never falling along the last dimension, each value on 1 to 48 neighbouring positions
- out_weight: bfloat16 [4, 8192, 8192], P('section', 'tensor', 'dp'), may hold values from -0.0625 to 0.0625
- stash_held: bfloat16 [4, 3, 1024, 20480], P('section', None, 'dp', 'tensor'), may hold values from -22 to 22, as said below
- len_bwd: int32 [4, 8, 8], P('section', 'dp'), may hold values from 1 to 48, 128 in all within a row
- out_grad: bfloat16 [4, 1024, 8192], P('section', ('dp', 'tensor')), may hold values from -6 to 6
- evict_slot: int32 [4], P('section'), may hold values from 0 to 2
- fetch_slot: int32 [4, 8], P('section', 'dp'), may hold values from 0 to 2
Outputs:
- layer_out: bfloat16 [4, 1024, 8192], P('section', ('dp', 'tensor'))
- stash_next: bfloat16 [4, 3, 1024, 20480], P('section', None, 'dp', 'tensor')
- weight_grad: bfloat16 [4, 8192, 8192], P('section', 'tensor', 'dp')
- attn_grad: bfloat16 [4, 1024, 12288], P('section', 'dp', 'tensor')
Inputs may be any that keep to these rules, and one draw needn't show every extreme that they name: `attn_in`: the blocks of one group hold equal keys and equal values. `stash_held`: the blocks of one group hold equal keys and equal values. `seg_fwd`: each run of 128 tokens holds 8 sequences, the longest exactly 48 tokens. `len_bwd`: each run's lengths sum to 128, the largest exactly 48.
All inputs are finite; a program needn't handle non-finite values.
Results may differ from a plain program's by a relative error of at most 0.02.
Values may be sent and summed in bfloat16 or wider, within the bound.
A program may use at most 64 MiB of HBM per device.

v0:
```python
import jax
import jax.numpy as jnp
from jax import lax
from jax.sharding import PartitionSpec as P

HEAD = 128


def from_partner(value, axis, apart):
    mask = 2**apart
    pairs = [(source, source ^ mask) for source in range(lax.axis_size(axis))]
    return lax.ppermute(value, axis, pairs)


def split_heads(packed, q_count, kv_count):
    tok_count = packed.shape[0]
    q_width = q_count * HEAD
    kv_width = kv_count * HEAD
    query_heads = packed[:, :q_width].reshape(tok_count, kv_count, q_count // kv_count, HEAD)
    key_heads = packed[:, q_width : q_width + kv_width].reshape(tok_count, kv_count, HEAD)
    value_heads = packed[:, q_width + kv_width : q_width + 2 * kv_width].reshape(
        tok_count, kv_count, HEAD
    )
    return (query_heads, key_heads, value_heads)


def probabilities(query_heads, key_heads, segment):
    scores = jnp.einsum(
        "tkgd,skd->kgts", query_heads, key_heads, preferred_element_type=jnp.float32
    ) * HEAD ** (-0.5)
    tok_count = segment.shape[0]
    position = lax.broadcasted_iota(jnp.int32, (tok_count, tok_count), 0)
    earlier = lax.broadcasted_iota(jnp.int32, (tok_count, tok_count), 1)
    allowed = (segment[:, None] == segment[None, :]) & (earlier <= position)
    masked = jnp.where(allowed, scores, -1e30)
    highest = jnp.max(masked, axis=-1, keepdims=True)
    raised = jnp.where(allowed, jnp.exp(masked - highest), 0.0)
    return raised / jnp.sum(raised, axis=-1, keepdims=True)


def attend(packed, segment, q_count, kv_count):
    query_heads, key_heads, value_heads = split_heads(packed, q_count, kv_count)
    weights = probabilities(query_heads, key_heads, segment).astype(jnp.bfloat16)
    result = jnp.einsum("kgts,skd->tkgd", weights, value_heads, preferred_element_type=jnp.float32)
    return result.astype(jnp.bfloat16).reshape(packed.shape[0], q_count * HEAD)


def attend_back(packed, segment, grad_out, q_count, kv_count):
    tok_count = packed.shape[0]
    query_heads, key_heads, value_heads = split_heads(packed, q_count, kv_count)
    width_in = (q_count + 2 * kv_count) * HEAD
    outputs = packed[:, width_in:].reshape(tok_count, kv_count, q_count // kv_count, HEAD)
    probs = probabilities(query_heads, key_heads, segment)
    weights = probs.astype(jnp.bfloat16)
    grad_heads = grad_out.reshape(tok_count, kv_count, q_count // kv_count, HEAD)
    grad_values = jnp.einsum(
        "kgts,tkgd->skd", weights, grad_heads, preferred_element_type=jnp.float32
    )
    grad_probs = jnp.einsum(
        "tkgd,skd->kgts", grad_heads, value_heads, preferred_element_type=jnp.float32
    )
    inner = jnp.sum(grad_heads.astype(jnp.float32) * outputs.astype(jnp.float32), axis=-1)
    inner = jnp.transpose(inner, (1, 2, 0))[..., None]
    grad_scores = (probs * (grad_probs - inner)).astype(jnp.bfloat16)
    grad_query = jnp.einsum(
        "kgts,skd->tkgd", grad_scores, key_heads, preferred_element_type=jnp.float32
    ) * HEAD ** (-0.5)
    grad_keys = jnp.einsum(
        "kgts,tkgd->skd", grad_scores, query_heads, preferred_element_type=jnp.float32
    ) * HEAD ** (-0.5)
    shared = jnp.concatenate(
        [
            grad_keys.reshape(tok_count, kv_count * HEAD),
            grad_values.reshape(tok_count, kv_count * HEAD),
        ],
        axis=1,
    )
    return (grad_query.astype(jnp.bfloat16).reshape(tok_count, q_count * HEAD), shared)


def lengths_to_segments(lengths, tok_count):
    ends = jnp.cumsum(lengths)
    position = lax.broadcasted_iota(jnp.int32, (tok_count, lengths.shape[0]), 0)
    return jnp.sum((position >= ends[None, :]).astype(jnp.int32), axis=1)


def body(
    resid_in, attn_in, seg_fwd, out_weight, stash_held, len_bwd, out_grad, evict_slot, fetch_slot
):
    packed = attn_in[0]
    tok_count = packed.shape[0]
    weight_local = out_weight[0]
    q_width = weight_local.shape[0]
    q_count = q_width // HEAD
    kv_count = (packed.shape[1] // HEAD - q_count) // 2
    held = stash_held[0]
    section_bits = lax.axis_size("section").bit_length() - 1
    returned = lax.dynamic_index_in_dim(held, fetch_slot[0, 0], 0, keepdims=False)
    attended = attend(packed, seg_fwd[0, 0], q_count, kv_count)
    evicted = jnp.concatenate([packed, attended], axis=1)
    for bit in range(section_bits):
        evicted, returned = from_partner((evicted, returned), "section", bit)
    slot_index = lax.broadcasted_iota(jnp.int32, (held.shape[0], 1, 1), 0)
    stash_next = jnp.where(slot_index == evict_slot[0], evicted[None], held)
    weight_full = lax.all_gather(weight_local, "dp", axis=1, tiled=True)
    branch = lax.psum_scatter(
        jnp.dot(attended, weight_full, preferred_element_type=jnp.float32).astype(jnp.bfloat16),
        "tensor",
        scatter_dimension=0,
        tiled=True,
    ).astype(jnp.float32)
    layer_out = (resid_in[0].astype(jnp.float32) + branch).astype(jnp.bfloat16)
    grad_tokens = lax.all_gather(out_grad[0], "tensor", axis=0, tiled=True)
    grad_columns = lax.all_to_all(grad_tokens, "dp", split_axis=1, concat_axis=0, tiled=True)
    old_outputs = returned[:, (q_count + 2 * kv_count) * HEAD :]
    all_outputs = lax.all_gather(old_outputs, "dp", axis=0, tiled=True)
    weight_grad = lax.dot_general(
        all_outputs, grad_columns, (((0,), (0,)), ((), ())), preferred_element_type=jnp.float32
    ).astype(jnp.bfloat16)
    head_grad = lax.dot_general(
        grad_tokens, weight_full, (((1,), (1,)), ((), ())), preferred_element_type=jnp.float32
    )
    head_grad = head_grad.astype(jnp.bfloat16)
    segment_old = lengths_to_segments(len_bwd[0, 0], tok_count)
    grad_query, shared = attend_back(returned, segment_old, head_grad, q_count, kv_count)
    bit = 0
    shared = shared + from_partner(shared.astype(jnp.bfloat16), "tensor", bit).astype(shared.dtype)
    attn_grad = jnp.concatenate([grad_query, shared.astype(jnp.bfloat16)], axis=1)
    return (layer_out[None], stash_next[None], weight_grad[None], attn_grad[None])


def solution(mesh):
    placed = (
        P("section", ("dp", "tensor"), None),
        P("section", "dp", "tensor"),
        P("section", "dp", None),
        P("section", "tensor", "dp"),
        P("section", None, "dp", "tensor"),
        P("section", "dp", None),
        P("section", ("dp", "tensor"), None),
        P("section"),
        P("section", "dp"),
    )
    return jax.shard_map(
        body,
        mesh=mesh,
        in_specs=placed,
        out_specs=(
            P("section", ("dp", "tensor"), None),
            P("section", None, "dp", "tensor"),
            P("section", "tensor", "dp"),
            P("section", "dp", "tensor"),
        ),
        check_vma=False,
    )
```

profile of v0, /device:TPU:16, one launch (start us, length us, event | category | flops | bytes accessed | tf_op | source)
XLA Modules:
  0.0 500.8 jit_solution(6367085611863125623)
XLA Ops:
  9.3 1.0 dynamic-slice_bitcast_fusion
  10.3 1.9 collective-permute-start.2
  12.3 1.6 collective-permute-done.2
  13.9 3.4 collective-permute-start.3
  17.3 8.2 %collective-permute-done.3 = bf16[128,1280]{1,0:T(8,128)(2,1)S(1)} collective-permute-done((bf16[128,1280]{1,0:T(8,128)(2,1)S(1)}, bf16[128,1280]{1,0:T(8,128)(2,1)S(1)}, u32[]{:S(2)}, u32[]{:S(2)}) %collective-permute-start.3) | collective-permute-done | bytes 327712 | tf_op jit(solution)/shard_map/ppermute | solution.py:12
  26.9 78.1 %all-gather.10.cloned.1.call-done = bf16[1,128,8192]{2,1,0:T(8,128)(2,1)} async-done(((bf16[1,8,8192]{2,1,0:T(8,128)(2,1)}), bf16[1,128,8192]{2,1,0:T(8,128)(2,1)}) %all-gather.10.cloned.1.call-update) | async-done | bytes 2097168 | tf_op jit(solution)/shard_map/all_gather | solution.py:113
  105.0 4.1 copy.80
  109.1 7.5 %all-to-all-start = ((bf16[128,8,1024]{0,2,1:T(8,128)(2,1)}), bf16[128,8,1024]{0,2,1:T(8,128)(2,1)S(1)}, u32[]{:S(2)}, u32[]{:S(2)}) async-start(bf16[128,8,1024]{0,2,1:T(8,128)(2,1)} %bitcast.140), calls=%async_computation.1 | async-start | bytes 4194304 | tf_op jit(solution)/shard_map/all_to_all | solution.py:114
  117.4 123.7 %all-gather.8.cloned.1.call-done = bf16[1,512,8192]{2,1,0:T(8,128)(2,1)} async-done(((bf16[1,512,1024]{2,1,0:T(8,128)(2,1)}), bf16[1,512,8192]{2,1,0:T(8,128)(2,1)}) %all-gather.8.cloned.1.call-update) | async-done | bytes 8388624 | tf_op jit(solution)/shard_map/all_gather | solution.py:105
  241.2 6.0 %convolution_convert_fusion = bf16[128,8192]{1,0:T(8,128)(2,1)} fusion(bf16[128,512]{0,1:T(8,128)(2,1)S(1)} %bitcast.150, bf16[1,512,8192]{2,1,0:T(8,128)(2,1)} %all-gather.8.cloned.1.call-done), kind=kOutput, calls=%fused_computation | convolution fusion | flops 1074790400 | bytes 10616832 | tf_op jit(solution)/shard_map/dot_general | solution.py:107
  247.2 1.1 copy.102
  249.0 2.0 collective-permute-start
  252.9 2.5 collective-permute-start.1
  255.5 0.9 fusion.38
  256.5 8.3 %collective-permute-done.1 = bf16[128,1280]{1,0:T(8,128)(2,1)} collective-permute-done((bf16[128,1280]{1,0:T(8,128)(2,1)}, bf16[128,1280]{1,0:T(8,128)(2,1)}, u32[]{:S(2)}, u32[]{:S(2)}) %collective-permute-start.1) | collective-permute-done | bytes 327712 | tf_op jit(solution)/shard_map/ppermute | solution.py:12
  264.8 2.1 broadcast_select_fusion
  266.9 2.6 copy.81
  269.6 11.6 %all-gather.6.cloned.1.call-done = bf16[1024,512]{1,0:T(8,128)(2,1)} async-done(((bf16[128,512]{1,0:T(8,128)(2,1)}), bf16[1024,512]{1,0:T(8,128)(2,1)}) %all-gather.6.cloned.1.call-update) | async-done | bytes 1048592 | tf_op jit(solution)/shard_map/all_gather | solution.py:116
  281.2 4.3 fusion.4
  285.5 6.4 %convert_multiply_fusion = (f32[128,512]{1,0:T(8,128)S(1)}, bf16[128,512]{1,0:T(8,128)(2,1)S(1)}) fusion(bf16[128,1280]{1,0:T(8,128)(2,1)S(1)} %copy-done.4, bf16[1,512,8192]{2,1,0:T(8,128)(2,1)} %all-gather.8.cloned.1.call-done, bf16[1,128,8192]{2,1,0:T(8,128)(2,1)S(1)} %copy-done), kind=kOutput, calls=%fused_computation.31 | convolution fusion | flops 1074003968 | bytes 11010048 | tf_op jit(solution)/shard_map/dot_general | solution.py:120
  293.0 3.4 collective-permute-start.4
  296.8 2.4 collective-permute-done.4
  300.0 192.6 %reduce-scatter.2.cloned.1.call-done = bf16[8,8192]{1,0:T(8,128)(2,1)} async-done(((bf16[128,8192]{1,0:T(8,128)(2,1)}), bf16[8,8192]{1,0:T(8,128)(2,1)}) %reduce-scatter.2.cloned.1.call-update) | async-done | bytes 131088 | tf_op jit(solution)/shard_map/reduce_scatter | solution.py:106
  492.7 1.6 fusion.25
  (55 shorter events, 8.1 us)
Async XLA Ops:
  7.2 97.9 %all-gather.10.cloned.1.call-start = ((), (), s32[]{:S(2)}) async-start(), calls=%async_computation.5 | async-start | bytes 2228224 | tf_op jit(solution)/shard_map/all_gather | solution.py:113
  7.9 233.3 %all-gather.8.cloned.1.call-start = ((), (), s32[]{:S(2)}) async-start(), calls=%async_computation.4 | async-start | bytes 9437184 | tf_op jit(solution)/shard_map/all_gather | solution.py:105
  8.6 272.5 %all-gather.6.cloned.1.call-start = ((), (), s32[]{:S(2)}) async-start(), calls=%async_computation.3 | async-start | bytes 1179648 | tf_op jit(solution)/shard_map/all_gather | solution.py:116
  10.3 3.5 collective-permute-start.2
  13.9 11.6 %collective-permute-start.3 = (bf16[128,1280]{1,0:T(8,128)(2,1)S(1)}, bf16[128,1280]{1,0:T(8,128)(2,1)S(1)}, u32[]{:S(2)}, u32[]{:S(2)}) collective-permute-start(bf16[128,1280]{1,0:T(8,128)(2,1)S(1)} %collective-permute-done.2), channel_id=1, source_target_pairs={{0,256},{128,384},{256,0},{384,128},{1,257},{129,385},{257,1},{385... | collective-permute-start | bytes 983048 | tf_op jit(solution)/shard_map/ppermute | solution.py:12
  25.5 0.7 copy-start.3
  109.1 7.6 %copy-start.2 = (bf16[1,128,768]{2,1,0:T(8,128)(2,1)S(1)}, bf16[1,128,768]{2,1,0:T(8,128)(2,1)}, u32[]{:S(2)}) copy-start(bf16[1,128,768]{2,1,0:T(8,128)(2,1)} %param.10) | copy-start | bytes 589828
  109.1 7.7 %copy-start.7 = (s32[1,1,128]{2,1,0:T(1,128)S(1)}, s32[1,1,128]{2,1,0:T(1,128)}, u32[]{:S(2)}) copy-start(s32[1,1,128]{2,1,0:T(1,128)} %param.11) | copy-start | bytes 1540
  109.1 157.9 %all-to-all-start = ((bf16[128,8,1024]{0,2,1:T(8,128)(2,1)}), bf16[128,8,1024]{0,2,1:T(8,128)(2,1)S(1)}, u32[]{:S(2)}, u32[]{:S(2)}) async-start(bf16[128,8,1024]{0,2,1:T(8,128)(2,1)} %bitcast.140), calls=%async_computation.1 | async-start | bytes 4194304 | tf_op jit(solution)/shard_map/all_to_all | solution.py:114
  116.6 376.0 %reduce-scatter.2.cloned.1.call-start = ((), (), s32[]{:S(2)}) async-start(), calls=%async_computation.2 | async-start | bytes 2228224 | tf_op jit(solution)/shard_map/reduce_scatter | solution.py:106
  117.4 129.8 %copy-start.5 = (bf16[4,128,128]{1,2,0:T(8,128)(2,1)}, bf16[4,128,128]{1,2,0:T(8,128)(2,1)S(1)}, u32[]{:S(2)}) copy-start(bf16[4,128,128]{1,2,0:T(8,128)(2,1)S(1)} %convolution_convert_fusion.2) | copy-start | bytes 393220
  247.2 3.8 copy-start.8
  247.2 17.7 %copy-start.1 = (bf16[1,3,128,1280]{3,2,1,0:T(8,128)(2,1)S(1)}, bf16[1,3,128,1280]{3,2,1,0:T(8,128)(2,1)}, u32[]{:S(2)}) copy-start(bf16[1,3,128,1280]{3,2,1,0:T(8,128)(2,1)} %param.13) | copy-start | bytes 2949124
  249.0 3.9 collective-permute-start
  252.9 12.0 %collective-permute-start.1 = (bf16[128,1280]{1,0:T(8,128)(2,1)}, bf16[128,1280]{1,0:T(8,128)(2,1)}, u32[]{:S(2)}, u32[]{:S(2)}) collective-permute-start(bf16[128,1280]{1,0:T(8,128)(2,1)} %collective-permute-done), channel_id=1, source_target_pairs={{0,256},{128,384},{256,0},{384,128},{1,257},{129,385},{257,1},{385... | collective-permute-start | bytes 983048 | tf_op jit(solution)/shard_map/ppermute | solution.py:12
  281.2 4.3 copy-start
  281.2 4.3 copy-start.4
  292.4 200.3 %copy-start.6 = (bf16[1,8,8192]{2,1,0:T(8,128)(2,1)S(1)}, bf16[1,8,8192]{2,1,0:T(8,128)(2,1)}, u32[]{:S(2)}) copy-start(bf16[1,8,8192]{2,1,0:T(8,128)(2,1)} %param.9) | copy-start | bytes 393220
  293.0 6.2 %collective-permute-start.4 = (bf16[128,256]{0,1:T(8,128)(2,1)S(1)}, bf16[128,256]{0,1:T(8,128)(2,1)S(1)}, u32[]{:S(2)}, u32[]{:S(2)}) collective-permute-start(bf16[128,256]{0,1:T(8,128)(2,1)S(1)} %fusion.30), channel_id=1, source_target_pairs={{0,1},{1,0},{2,3},{3,2},{4,5},{5,4},{6,7},{7,6},{8,9},{9,8},{10,11... | collective-permute-start | bytes 196616 | tf_op jit(solution)/shard_map/ppermute | solution.py:12
Sparse Core Ops, SparseCore 0:
  11.2 93.8 all-gather.9
  107.1 133.9 all-gather.7
  243.8 37.3 all-gather.5
  285.5 207.1 reduce-scatter.1
where the time goes:
time: 501 us
  waiting for transfers between devices  428 us (85%)
  starting transfers between devices  20.8 us (4%)
  matrix products  18.9 us (4%)
  between operations  15.3 us (3%)
  local copies, waits for them, and re-layouts  10.9 us (2%)
  other arithmetic  6.44 us (1%)
    reduce_scatter x1, waiting for transfers between devices, body(): lax.psum_scatter(jnp.dot(attended, weight_full, preferred_element_type=jn...  193 us
    all_gather x1, waiting for transfers between devices, body(): weight_full = lax.all_gather(weight_local, 'dp', axis=1, tiled=True)  124 us
    all_gather x1, waiting for transfers between devices, body(): grad_tokens = lax.all_gather(out_grad[0], 'tensor', axis=0, tiled=True)  78.1 us
    ppermute x5, waiting for transfers between devices, from_partner(): return lax.ppermute(value, axis, pairs)  21 us
    ppermute x5, starting transfers between devices, from_partner(): return lax.ppermute(value, axis, pairs)  13.1 us
    all_gather x1, waiting for transfers between devices, body(): all_outputs = lax.all_gather(old_outputs, 'dp', axis=0, tiled=True)  11.6 us
  transfers between devices with their start and end apart: 10, of which 9 were waited for; matrix products, arithmetic and copies ran while one was open for 7% of the time, Pallas kernels for 0%

commit v1 on v0

v1 whole, which is shorter than its diff:
```python
import functools

import jax
import jax.numpy as jnp
from jax import lax
from jax.experimental import pallas as pl
from jax.experimental.pallas import tpu as pltpu
from jax.sharding import PartitionSpec as P

HEAD = 128
ROWS = 8
MESH = pl.DeviceIdType.MESH
F32 = jnp.float32
BF16 = jnp.bfloat16
SEMS = 128


def dot(a, b, ca=1, cb=0):
    return lax.dot_general(a, b, (((ca,), (cb,)), ((), ())), preferred_element_type=F32)


def streams(n):
    h = n // 2
    return [s for s in ((1, 0, h), (-1, 1, h), (1, 1, h - 1), (-1, 0, h - 1)) if s[2] > 0]


def probabilities(q, k, allowed, heads):
    tok = k.shape[0]
    scores = dot(q, k, 1, 1).reshape(heads, tok, tok) * HEAD ** (-0.5)
    masked = jnp.where(allowed[None], scores, -1e30)
    highest = jnp.max(masked, axis=-1, keepdims=True)
    raised = jnp.where(allowed[None], jnp.exp(masked - highest), 0.0)
    return (raised / jnp.sum(raised, axis=-1, keepdims=True)).reshape(heads * tok, tok)


def stack_heads(x, heads):
    return jnp.concatenate([x[:, h * HEAD : (h + 1) * HEAD] for h in range(heads)], axis=0)


def unstack_heads(x, heads):
    tok = x.shape[0] // heads
    return jnp.concatenate([x[h * tok : (h + 1) * tok] for h in range(heads)], axis=1)


def to_tall(x):
    half = x.shape[1] // 2
    return jnp.concatenate([x[:, :half], x[:, half:]], axis=0)


def to_wide(x):
    return jnp.concatenate([x[:ROWS], x[ROWS:]], axis=1)


class Copies:
    def __init__(self, send_sems, recv_sems):
        self.send_sems, self.recv_sems = send_sems, recv_sems
        self.count = 0
        self.started = []

    def make(self, src, dst, device):
        i = self.count
        self.count += 1
        assert i < SEMS
        return pltpu.make_async_remote_copy(
            src_ref=src,
            dst_ref=dst,
            send_sem=self.send_sems.at[i],
            recv_sem=self.recv_sems.at[i],
            device_id=device,
            device_id_type=MESH,
        )

    def send(self, src, dst, device):
        copy = self.make(src, dst, device)
        copy.start()
        self.started.append(copy)
        return copy

    def finish(self):
        for copy in self.started:
            copy.wait_send()


class Gather:
    def __init__(self, copies, n, me, device, place):
        self.copies, self.n, self.me = copies, n, me
        self.device, self.place = device, place
        self.streams = streams(n)
        self.moves = {}

    def step(self, r, halves=(0, 1)):
        for half in halves:
            for way, h, hops in self.streams:
                if h != half:
                    continue
                if 1 <= r <= hops:
                    self.moves[(way, h, r - 1)].wait_recv()
                if r < hops:
                    origin = (self.me - way * r + self.n) % self.n
                    ref = self.place(origin, h)
                    to = (self.me + way + self.n) % self.n
                    self.moves[(way, h, r)] = self.copies.send(ref, ref, self.device(to))


class Reduce:
    def __init__(self, copies, n, me, device, slots):
        self.copies, self.n, self.me = copies, n, me
        self.device, self.slots = device, slots
        self.streams = streams(n)
        self.h = n // 2
        self.moves = {}

    def slot(self, way, half, r):
        return self.slots.at[0 if way == 1 else 1, half, r]

    def step(self, r, own):
        for way, half, hops in self.streams:
            first = self.h - hops
            if r < first:
                continue
            ref = self.slot(way, half, r)
            value = own(way, half)
            if r > first:
                self.moves[(way, half, r - 1)].wait_recv()
                value = value + ref[...].astype(F32)
            ref[...] = value.astype(BF16)
            to = (self.me + way + self.n) % self.n
            self.moves[(way, half, r)] = self.copies.send(
                ref, self.slot(way, half, r + 1), self.device(to)
            )

    def last(self, half):
        total = None
        for way, h, hops in self.streams:
            if h != half:
                continue
            self.moves[(way, h, self.h - 1)].wait_recv()
            part = self.slot(way, h, self.h)[...].astype(F32)
            total = part if total is None else total + part
        return total


def kernel(
    dims,
    resid,
    attn_in,
    seg,
    lens,
    weight_hbm,
    stash_hbm,
    out_grad,
    evict,
    fetch,
    lay_out,
    stash_out,
    wgrad_out,
    agrad_out,
    weight,
    stash,
    b1s,
    b1r,
    G,
    part,
    zslots,
    A,
    O,
    yslots,
    xs,
    xr,
    f5s,
    f5r,
    attb,
    reto,
    retq,
    retr,
    evp,
    eva,
    shs,
    shr,
    OT,
    wgv,
    send_sems,
    recv_sems,
    local_sems,
):
    n_sec, nz, nt = dims
    ny = nt // 2
    tok = nt * ROWS
    C = weight.shape[1]
    QW = weight.shape[0]
    heads = QW // HEAD
    W_IN = QW + 2 * HEAD

    sec = lax.axis_index("section")
    z = lax.axis_index("dp")
    t = lax.axis_index("tensor")
    xh = t // ny
    y = t % ny
    mirror = {"section": n_sec - 1 - sec}
    xpeer = {"tensor": (1 - xh) * ny + y}
    pair = {"tensor": t + 1 - 2 * (t % 2)}

    def zdev(i):
        return {"dp": i}

    def ydev(i):
        return {"tensor": xh * ny + i}

    barrier = pltpu.get_barrier_semaphore()
    greeted = [zdev((z + k) % nz) for k in range(1, nz)]
    greeted += [ydev((y + 1) % ny), ydev((y + ny - 1) % ny)] + [xpeer, mirror]
    for device in greeted:
        pl.semaphore_signal(barrier, inc=1, device_id=device, device_id_type=MESH)

    load_weight = pltpu.make_async_copy(weight_hbm, weight, local_sems.at[0])
    load_stash = pltpu.make_async_copy(stash_hbm, stash, local_sems.at[1])
    load_stash.start()
    load_weight.start()

    copies = Copies(send_sems, recv_sems)

    for d in range(nz):
        b1s[d] = to_tall(out_grad[:, d * C : (d + 1) * C].astype(F32)).astype(BF16)
    b1r[z] = b1s[z]

    pl.semaphore_wait(barrier, len(greeted))

    b1 = []
    for k in range(1, nz):
        d = (z + k) % nz
        b1.append(copies.send(b1s.at[d], b1r.at[z], zdev(d)))

    def permuted(x):
        return [
            jnp.concatenate(
                [x[h * ny * ROWS + b * ROWS : h * ny * ROWS + (b + 1) * ROWS] for h in (0, 1)],
                axis=0,
            )
            for b in range(ny)
        ]

    def natural(x):
        return jnp.concatenate(
            [x[(2 * b + h) * ROWS : (2 * b + h + 1) * ROWS] for h in (0, 1) for b in range(ny)],
            axis=0,
        )

    load_stash.wait()
    slot = fetch[0, 0]
    held = stash[slot]
    for b, rows in enumerate(permuted(held[:, W_IN:].astype(F32))):
        reto[b] = rows.astype(BF16)
    retq[...] = held[:, :W_IN]
    move_ret_o = copies.send(reto, O.at[:, z], mirror)

    row_id = lax.broadcasted_iota(jnp.int32, (tok, tok), 0)
    col_id = lax.broadcasted_iota(jnp.int32, (tok, tok), 1)
    seg_cols = jnp.broadcast_to(seg[...].astype(F32), (tok, tok))
    allowed = (seg_cols == jnp.transpose(seg_cols)) & (col_id <= row_id)
    q = stack_heads(attn_in[:, :QW], heads)
    k = attn_in[:, QW : QW + HEAD]
    v = attn_in[:, QW + HEAD : W_IN]
    weights = probabilities(q, k, allowed, heads).astype(BF16)
    att = unstack_heads(dot(weights, v), heads)
    attb[...] = att.astype(BF16)
    for b, rows in enumerate(permuted(att)):
        A[b, z] = rows.astype(BF16)

    hy = ny // 2
    gather_a = Gather(copies, nz, z, zdev, lambda o, h: A.at[pl.ds(h * hy, hy), o])
    gather_o = Gather(copies, nz, z, zdev, lambda o, h: O.at[pl.ds(h * hy, hy), o])
    gather_g = Gather(copies, ny, y, ydev, lambda o, h: G.at[o, xh if h == 0 else 1 - xh])
    reduce_z = Reduce(copies, nz, z, zdev, zslots)
    reduce_y = Reduce(copies, ny, y, ydev, yslots)

    gather_a.step(0)

    for copy in b1:
        copy.wait_recv()
    for p in range(nz // 2):
        rows = [to_wide(b1r[2 * p + j].astype(F32)) for j in (0, 1)]
        G[y, xh, pl.ds(2 * ROWS * p, 2 * ROWS), :] = jnp.concatenate(rows, axis=0).astype(BF16)
    move_g = copies.send(G.at[y, xh], G.at[y, xh], xpeer)
    gather_g.step(0, (0,))
    move_g.wait_recv()
    gather_g.step(0, (1,))

    move_ret_q = copies.send(retq, retr, mirror)
    move_ev_p = copies.send(attn_in, evp, mirror)
    move_ev_a = copies.send(attb, eva, mirror)
    load_weight.wait()

    def head_grad_part(b):
        res = dot(G[b].reshape(2 * nz * ROWS, C), weight[...], 1, 1)
        for d in range(nz):
            pair_rows = [res[(h * nz + d) * ROWS : (h * nz + d + 1) * ROWS] for h in (0, 1)]
            part[d, b] = jnp.concatenate(pair_rows, axis=0).astype(BF16)

    def branch_part(b):
        return dot(A[b].reshape(2 * nz * ROWS, QW), weight[...])

    def at_y(way, r):
        return (y + way * r + ny) % ny

    def at_z(way, r):
        return (z + way * r + nz) % nz

    def head_grad_step(r):
        def own(way, half):
            return part[at_z(way, nz // 2 - r), pl.ds(half * hy, hy)].astype(F32)

        reduce_z.step(r, own)

    half_rows = nz * ROWS

    def branch_step(r):
        parts = {1: branch_part(at_y(1, hy - r))}
        parts[-1] = branch_part(at_y(-1, hy - r)) if r > 0 else parts[1]

        def own(way, half):
            return parts[way][half * half_rows : (half + 1) * half_rows]

        reduce_y.step(r, own)

    hz = nz // 2
    head_grad_part(y)
    gather_a.step(1)
    move_ret_o.wait_recv()
    gather_o.step(0)
    for r in range(1, hy):
        gather_g.step(r)
        if r + 1 <= hz:
            gather_a.step(r + 1)
        if r <= hz:
            gather_o.step(r)
        head_grad_part(at_y(1, r))
        head_grad_part(at_y(-1, r))
    for r in range(hy + 1, hz + 1):
        gather_a.step(r)
    branch_step(0)
    for r in range(hy, hz + 1):
        gather_o.step(r)
    gather_g.step(hy)
    head_grad_part(at_y(1, hy))

    def weight_grad_part(i):
        cols = pl.ds(i * (C // 4), C // 4)
        wgv[:, cols] = dot(OT[...], G[:, :, :, cols].reshape(nt * nz * ROWS, C // 4)).astype(BF16)

    def arrange_outputs():
        for b in range(ny):
            x = O[b].astype(F32)
            rows = [x[d, h * ROWS : (h + 1) * ROWS] for h in (0, 1) for d in range(nz)]
            block = jnp.concatenate(rows, axis=0)
            width = 2 * nz * ROWS
            OT[:, b * width : (b + 1) * width] = jnp.transpose(block).astype(BF16)

    head_grad_step(0)
    arrange_outputs()
    for r in range(1, max(hy, hz)):
        if r < hz:
            head_grad_step(r)
        if r < hy:
            branch_step(r)
        weight_grad_part(r - 1)
    for i in range(max(hy, hz) - 1, 4):
        weight_grad_part(i)
    store_wgrad = pltpu.make_async_copy(wgv, wgrad_out, local_sems.at[2])
    store_wgrad.start()

    halves = []
    for h in (0, 1):
        own = part[z, pl.ds(h * hy, hy)].astype(F32)
        halves.append((own + reduce_z.last(h)).reshape(hy * 2 * ROWS, QW))
    d_out = natural(jnp.concatenate(halves, axis=0)).astype(BF16)
    old = natural(O[:, z].astype(F32).reshape(tok, QW))
    move_ret_q.wait_recv()
    end = jnp.int32(0)
    seg_row = jnp.zeros((tok, tok), jnp.int32)
    seg_col = jnp.zeros((tok, tok), jnp.int32)
    for c in range(lens.shape[1]):
        end = end + lens[0, c]
        seg_row += (row_id >= end).astype(jnp.int32)
        seg_col += (col_id >= end).astype(jnp.int32)
    allowed = (seg_row == seg_col) & (col_id <= row_id)
    q = stack_heads(retr[:, :QW], heads)
    k = retr[:, QW : QW + HEAD]
    v = retr[:, QW + HEAD : W_IN]
    probs = probabilities(q, k, allowed, heads)
    d_heads = stack_heads(d_out, heads)
    grad_v = dot(probs.astype(BF16), d_heads, 0, 0)
    grad_p = dot(d_heads, v, 1, 1)
    inner = jnp.sum(d_heads.astype(F32) * stack_heads(old, heads), axis=-1, keepdims=True)
    grad_s = (probs * (grad_p - inner)).astype(BF16)
    grad_k = dot(grad_s, q, 0, 0) * HEAD ** (-0.5)
    shs[:, :HEAD] = grad_k.astype(BF16)
    shs[:, HEAD:] = grad_v.astype(BF16)
    move_shared = copies.send(shs, shr, pair)
    grad_q = dot(grad_s, k) * HEAD ** (-0.5)
    agrad_out[:, :QW] = unstack_heads(grad_q, heads).astype(BF16)

    mine = branch_part(y)
    sums = [mine[h * half_rows : (h + 1) * half_rows] + reduce_y.last(h) for h in (0, 1)]
    total = jnp.concatenate(sums, axis=0)

    def of_half(h):
        return jnp.concatenate(
            [total[(2 * d + h) * ROWS : (2 * d + h + 1) * ROWS] for d in range(nz)], axis=0
        )

    low, high = of_half(0), of_half(1)
    xs[...] = jnp.where(xh == 0, high, low).astype(BF16)
    move_x = copies.send(xs, xr, xpeer)
    keep = jnp.where(xh == 0, low, high)

    move_ev_p.wait_recv()
    move_ev_a.wait_recv()
    for i in range(stash.shape[0]):
        here = evict[0] == i
        stash[i, :, :W_IN] = jnp.where(here, evp[...], stash[i, :, :W_IN])
        stash[i, :, W_IN:] = jnp.where(here, eva[...], stash[i, :, W_IN:])
    store_stash = pltpu.make_async_copy(stash, stash_out, local_sems.at[3])
    store_stash.start()

    move_x.wait_recv()
    keep = keep + xr[...].astype(F32)
    for d in range(nz):
        f5s[d] = to_tall(keep[d * ROWS : (d + 1) * ROWS]).astype(BF16)
    f5r[z] = f5s[z]
    f5 = []
    for kk in range(1, nz):
        d = (z + kk) % nz
        f5.append(copies.send(f5s.at[d], f5r.at[z], zdev(d)))

    move_shared.wait_recv()
    agrad_out[:, QW:] = (shs[...].astype(F32) + shr[...].astype(F32)).astype(BF16)

    for copy in f5:
        copy.wait_recv()
    for d in range(nz):
        cols = slice(d * C, (d + 1) * C)
        lay_out[:, cols] = (resid[:, cols].astype(F32) + to_wide(f5r[d].astype(F32))).astype(BF16)

    copies.finish()
    store_wgrad.wait()
    store_stash.wait()


def body(
    dims,
    resid_in,
    attn_in,
    seg_fwd,
    out_weight,
    stash_held,
    len_bwd,
    out_grad,
    evict_slot,
    fetch_slot,
):
    n_sec, nz, nt = dims
    ny = nt // 2
    tok = nt * ROWS
    QW, C = out_weight.shape[1:]
    D = resid_in.shape[-1]
    W_IN = QW + 2 * HEAD
    slots, width = stash_held.shape[1], stash_held.shape[-1]
    vmem, smem, anywhere = (
        pl.BlockSpec(memory_space=s) for s in (pltpu.VMEM, pltpu.SMEM, pl.ANY)
    )

    def buf(*shape):
        return pltpu.VMEM(shape, BF16)

    outs = pl.pallas_call(
        functools.partial(kernel, dims),
        out_shape=(
            jax.ShapeDtypeStruct((ROWS, D), BF16),
            jax.ShapeDtypeStruct((slots, tok, width), BF16),
            jax.ShapeDtypeStruct((QW, C), BF16),
            jax.ShapeDtypeStruct((tok, W_IN), BF16),
        ),
        in_specs=[vmem, vmem, vmem, smem, anywhere, anywhere, vmem, smem, smem],
        out_specs=(vmem, anywhere, anywhere, vmem),
        scratch_shapes=[
            buf(QW, C),
            buf(slots, tok, width),
            buf(nz, 2 * ROWS, C // 2),
            buf(nz, 2 * ROWS, C // 2),
            buf(ny, 2, nz * ROWS, C),
            buf(nz, ny, 2 * ROWS, QW),
            buf(2, 2, nz // 2 + 1, ny // 2, 2 * ROWS, QW),
            buf(ny, nz, 2 * ROWS, QW),
            buf(ny, nz, 2 * ROWS, QW),
            buf(2, 2, ny // 2 + 1, nz * ROWS, C),
            buf(nz * ROWS, C),
            buf(nz * ROWS, C),
            buf(nz, 2 * ROWS, C // 2),
            buf(nz, 2 * ROWS, C // 2),
            buf(tok, QW),
            buf(ny, 2 * ROWS, QW),
            buf(tok, W_IN),
            buf(tok, W_IN),
            buf(tok, W_IN),
            buf(tok, QW),
            buf(tok, 2 * HEAD),
            buf(tok, 2 * HEAD),
            buf(QW, nt * nz * ROWS),
            buf(QW, C),
            pltpu.SemaphoreType.DMA((SEMS,)),
            pltpu.SemaphoreType.DMA((SEMS,)),
            pltpu.SemaphoreType.DMA((4,)),
        ],
        compiler_params=pltpu.CompilerParams(
            collective_id=0, has_side_effects=True, vmem_limit_bytes=48 * 2**20
        ),
    )(
        resid_in[0],
        attn_in[0],
        seg_fwd[0],
        len_bwd[0],
        out_weight[0],
        stash_held[0],
        out_grad[0],
        evict_slot,
        fetch_slot,
    )
    return tuple(x[None] for x in outs)


def solution(mesh):
    dims = tuple(mesh.shape[a] for a in ("section", "dp", "tensor"))
    placed = (
        P("section", ("dp", "tensor"), None),
        P("section", "dp", "tensor"),
        P("section", "dp", None),
        P("section", "tensor", "dp"),
        P("section", None, "dp", "tensor"),
        P("section", "dp", None),
        P("section", ("dp", "tensor"), None),
        P("section"),
        P("section", "dp"),
    )
    return jax.shard_map(
        functools.partial(body, dims),
        mesh=mesh,
        in_specs=placed,
        out_specs=(
            P("section", ("dp", "tensor"), None),
            P("section", None, "dp", "tensor"),
            P("section", "tensor", "dp"),
            P("section", "dp", "tensor"),
        ),
        check_vma=False,
    )
```

time: 501 us -> 92.4 us (0.18)
  the two profiles are of different devices: /device:TPU:16 before, /device:TPU:20 now
where the time goes in v1:
time: 92.4 us; the launch traced here: 92.2 us
  Pallas kernels  81.1 us (88%)
  local copies, waits for them, and re-layouts  9.06 us (10%)
  between operations  1.96 us (2%)
    pallas_call x1, Pallas kernels, body(): pl.pallas_call(functools.partial(kernel, dims), out_shape=(jax.ShapeDtype...  81.1 us
    unnamed x18, local copies, waits for them, and re-layouts  9.06 us

profile of v1, /device:TPU:20, one launch (start us, length us, event | category | flops | bytes accessed | tf_op | source)
XLA Modules:
  0.0 92.2 jit_solution(6930704734122477117)
XLA Ops:
  1.9 0.0 copy-start.5
  1.9 0.0 copy-start.6
  1.9 0.6 copy-done.5
  2.6 0.0 copy-done.6
  2.6 0.0 copy-start
  2.6 1.2 %copy-done = bf16[1,512,1024]{2,1,0:T(8,128)(2,1)S(1)} copy-done((bf16[1,512,1024]{2,1,0:T(8,128)(2,1)S(1)}, bf16[1,512,1024]{2,1,0:T(8,128)(2,1)}, u32[]{:S(2)}) %copy-start) | copy-done | bytes 1048600
  3.8 0.0 copy-start.1
  3.8 1.2 %copy-done.1 = bf16[1,3,128,1280]{3,2,1,0:T(8,128)(2,1)S(1)} copy-done((bf16[1,3,128,1280]{3,2,1,0:T(8,128)(2,1)S(1)}, bf16[1,3,128,1280]{3,2,1,0:T(8,128)(2,1)}, u32[]{:S(2)}) %copy-start.1) | copy-done | bytes 983064
  5.0 0.0 copy-start.2
  5.0 0.9 %copy-done.2 = bf16[1,128,768]{2,1,0:T(8,128)(2,1)S(1)} copy-done((bf16[1,128,768]{2,1,0:T(8,128)(2,1)S(1)}, bf16[1,128,768]{2,1,0:T(8,128)(2,1)}, u32[]{:S(2)}) %copy-start.2) | copy-done | bytes 196632
  6.0 0.0 copy-start.3
  6.0 0.9 copy-done.3
  6.9 0.0 copy-start.4
  6.9 0.9 copy-done.4
  7.8 81.1 %shard_map.120 = (bf16[8,8192]{1,0:T(8,128)(2,1)S(1)}, bf16[3,128,1280]{2,1,0:T(8,128)(2,1)S(1)}, bf16[512,1024]{1,0:T(8,128)(2,1)S(1)}, bf16[128,768]{1,0:T(8,128)(2,1)S(1)}) custom-call(bf16[8,8192]{1,0:T(8,128)(2,1)S(1)} %bitcast.17, bf16[128,768]{1,0:T(8,128)(2,1)S(1)} %bitcast.15, s32[1,128]{1,0:T(1,128)S(1)} %bitcast.20, s32[1,8]{1,0:T(1,128)S(1)} %bitcast.21, ...), custom_call_target="tpu_custom_call" | custom-call | tf_op jit(solution)/shard_map/pallas_call | solution.py:475
  88.9 0.7 copy.19
  89.6 0.9 %copy.20 = bf16[1,3,128,1280]{3,2,1,0:T(8,128)(2,1)} copy(bf16[1,3,128,1280]{3,2,1,0:T(8,128)(2,1)S(1)} %bitcast.14) | data formatting | bytes 1966080
  90.5 1.0 %copy.21 = bf16[1,512,1024]{2,1,0:T(8,128)(2,1)} copy(bf16[1,512,1024]{2,1,0:T(8,128)(2,1)S(1)} %bitcast.12) | data formatting | bytes 2097152
  91.5 0.7 copy.22
Async XLA Ops:
  1.9 0.7 copy-start.5
  1.9 0.7 copy-start.6
  2.6 1.2 %copy-start = (bf16[1,512,1024]{2,1,0:T(8,128)(2,1)S(1)}, bf16[1,512,1024]{2,1,0:T(8,128)(2,1)}, u32[]{:S(2)}) copy-start(bf16[1,512,1024]{2,1,0:T(8,128)(2,1)} %param.12) | copy-start | bytes 3145732
  3.8 1.2 %copy-start.1 = (bf16[1,3,128,1280]{3,2,1,0:T(8,128)(2,1)S(1)}, bf16[1,3,128,1280]{3,2,1,0:T(8,128)(2,1)}, u32[]{:S(2)}) copy-start(bf16[1,3,128,1280]{3,2,1,0:T(8,128)(2,1)} %param.13) | copy-start | bytes 2949124
  5.0 0.9 %copy-start.2 = (bf16[1,128,768]{2,1,0:T(8,128)(2,1)S(1)}, bf16[1,128,768]{2,1,0:T(8,128)(2,1)}, u32[]{:S(2)}) copy-start(bf16[1,128,768]{2,1,0:T(8,128)(2,1)} %param.10) | copy-start | bytes 589828
  6.0 0.9 copy-start.3
  6.9 0.9 copy-start.4

commit v2 on v1

v2 whole, which is shorter than its diff:
```python
import functools

import jax
import jax.numpy as jnp
from jax import lax
from jax.experimental import pallas as pl
from jax.experimental.pallas import tpu as pltpu
from jax.sharding import PartitionSpec as P

HEAD = 128
ROWS = 8
MESH = pl.DeviceIdType.MESH
F32 = jnp.float32
BF16 = jnp.bfloat16
SEMS = 160


def dot(a, b, ca=1, cb=0):
    return lax.dot_general(a, b, (((ca,), (cb,)), ((), ())), preferred_element_type=F32)


def probabilities(q, k, allowed, heads):
    tok = k.shape[0]
    scores = dot(q, k, 1, 1).reshape(heads, tok, tok) * HEAD ** (-0.5)
    masked = jnp.where(allowed[None], scores, -1e30)
    highest = jnp.max(masked, axis=-1, keepdims=True)
    raised = jnp.where(allowed[None], jnp.exp(masked - highest), 0.0)
    return (raised / jnp.sum(raised, axis=-1, keepdims=True)).reshape(heads * tok, tok)


def stack_heads(x, heads):
    return jnp.concatenate([x[:, h * HEAD : (h + 1) * HEAD] for h in range(heads)], axis=0)


def unstack_heads(x, heads):
    tok = x.shape[0] // heads
    return jnp.concatenate([x[h * tok : (h + 1) * tok] for h in range(heads)], axis=1)


def to_tall(x):
    half = x.shape[1] // 2
    return jnp.concatenate([x[:, :half], x[:, half:]], axis=0)


def to_wide(x):
    return jnp.concatenate([x[:ROWS], x[ROWS:]], axis=1)


class Pool:
    def __init__(self, sems):
        self.sems, self.count = sems, 0

    def new(self):
        assert self.count < SEMS
        self.count += 1
        return self.sems.at[self.count - 1]


class Sends:
    def __init__(self, pool, view, device):
        self.pool, self.view, self.device = pool, view, device
        self.sem = pool.new()

    def send(self, src, dst, device, recv=None):
        copy = pltpu.make_async_remote_copy(
            src_ref=src,
            dst_ref=dst,
            send_sem=self.sem,
            recv_sem=self.pool.new() if recv is None else recv,
            device_id=device,
            device_id_type=MESH,
        )
        copy.start()
        return copy

    def whole(self, recv=None):
        return pltpu.make_async_remote_copy(
            src_ref=self.view,
            dst_ref=self.view,
            send_sem=self.sem,
            recv_sem=self.sem if recv is None else recv,
            device_id=self.device,
            device_id_type=MESH,
        )

    def finish(self):
        self.whole().wait_send()


class Gather:
    def __init__(self, sends, n, me, device, streams, source, target):
        self.sends, self.n, self.me, self.device = sends, n, me, device
        self.streams, self.source, self.target = streams, source, target
        self.moves = {}

    def step(self, r, parts=None):
        for way, part, hops in self.streams:
            if parts is not None and part not in parts:
                continue
            if 1 <= r <= hops:
                self.moves[(way, part, r - 1)].wait_recv()
            if r < hops:
                to = (self.me + way + self.n) % self.n
                self.moves[(way, part, r)] = self.sends.send(
                    self.source(way, part, r), self.target(way, part, r), self.device(to)
                )


class RingSum:
    def __init__(self, sends, me, n, device, slot, parts):
        self.sends, self.me, self.n, self.device = sends, me, n, device
        self.slot, self.parts = slot, parts
        self.moves, self.terms = {}, {}

    def hops(self, side, p):
        return 4 if (p < len(self.parts) // 2) == (side == 0) else 3

    def step(self, r, term, parts=None):
        for p, (lo, count) in enumerate(self.parts):
            if parts is not None and p not in parts:
                continue
            for side, way in enumerate((1, -1)):
                first = 4 - self.hops(side, p)
                if r < first:
                    continue
                rel = 4 if r == 0 else way * (4 - r)
                if rel not in self.terms:
                    self.terms[rel] = term(rel)
                value = self.terms[rel][lo : lo + count]
                here = self.slot(side, r).at[pl.ds(lo, count)]
                there = self.slot(side, r + 1).at[pl.ds(lo, count)]
                if r > first:
                    self.moves[(side, p, r - 1)].wait_recv()
                    value = value + here[...].astype(F32)
                here[...] = value.astype(BF16)
                to = self.device((self.me + way + self.n) % self.n)
                self.moves[(side, p, r)] = self.sends.send(here, there, to)

    def last(self):
        for p in range(len(self.parts)):
            for side in (0, 1):
                self.moves[(side, p, 3)].wait_recv()
        return self.slot(0, 4)[...].astype(F32) + self.slot(1, 4)[...].astype(F32)


NEAR = (0, 1, -1, 2, -2, 3, -3, 4)
FAR = (4, 3, -3, 2, -2, 1, -1, 0)
A_PARTS, O_PARTS, G_PARTS = 2, 2, 4
X_HOPS = 2


def kernel(
    dims,
    resid_hbm,
    attn_in_hbm,
    seg_hbm,
    lens_hbm,
    weight_hbm,
    stash_hbm,
    out_grad_hbm,
    evict,
    fetch,
    lay_out,
    stash_out,
    wgrad_out,
    agrad_out,
    resid,
    attn_in,
    seg,
    lens,
    weight,
    stash,
    out_grad,
    b1s,
    b1r,
    G,
    part,
    zslots,
    A,
    O,
    yslots,
    f5s,
    f5r,
    xs,
    xr,
    attb,
    reto,
    reto_via,
    retq,
    retq_via,
    retr,
    evp_via,
    evp,
    eva_via,
    eva,
    shs,
    shr,
    OT,
    dnat,
    sems,
    local_sems,
):
    n_sec, nz, nt = dims
    ny = nt // 2
    tok = nt * ROWS
    C = weight.shape[1]
    QW = weight.shape[0]
    heads = QW // HEAD
    W_IN = QW + 2 * HEAD

    sec = lax.axis_index("section")
    z = lax.axis_index("dp")
    t = lax.axis_index("tensor")
    xh = t // ny
    y = t % ny
    other_core = {"section": sec + 1 - 2 * (sec % 2)}
    next_chip = {"section": (sec + n_sec // 2) % n_sec}
    xpeer = {"tensor": (1 - xh) * ny + y}
    pair = {"tensor": t + 1 - 2 * (t % 2)}

    def zdev(i):
        return {"dp": i}

    def ydev(i):
        return {"tensor": xh * ny + i}

    def xdev(i):
        return {"dp": i, "tensor": (1 - xh) * ny + y}

    def at_y(rel):
        return (y + rel + ny) % ny

    def at_z(rel):
        return (z + rel + nz) % nz

    barrier = pltpu.get_barrier_semaphore()
    greeted = [zdev(at_z(k)) for k in range(1, nz)]
    greeted += [xpeer]
    greeted += [ydev(at_y(1)), ydev(at_y(-1)), other_core, next_chip]
    for device in greeted:
        pl.semaphore_signal(barrier, inc=1, device_id=device, device_id_type=MESH)

    pairs = [
        (out_grad_hbm, out_grad),
        (stash_hbm, stash),
        (attn_in_hbm, attn_in),
        (seg_hbm, seg),
        (weight_hbm, weight),
        (lens_hbm, lens),
        (resid_hbm, resid),
    ]
    loads = [pltpu.make_async_copy(a, b, local_sems.at[i]) for i, (a, b) in enumerate(pairs)]
    for load in loads:
        load.start()
    loads[0].wait()

    pool = Pool(sems)
    groups = []

    def sends(view, device):
        groups.append(Sends(pool, view, device))
        return groups[-1]

    for d in range(nz):
        b1s[d] = to_tall(out_grad[:, d * C : (d + 1) * C].astype(F32)).astype(BF16)
    b1r[z] = b1s[z]

    pl.semaphore_wait(barrier, len(greeted))

    some_z = zdev(at_z(1))
    some_y = ydev(at_y(1))
    b1 = sends(b1r.at[pl.ds(0, nz - 1)], some_z)
    b1_recv = pool.new()
    for k in (4, 3, -3, 2, -2, 1, -1):
        b1.send(b1s.at[at_z(k)], b1r.at[z], zdev(at_z(k)), b1_recv)

    def permuted(x):
        return [
            jnp.concatenate(
                [x[h * ny * ROWS + b * ROWS : h * ny * ROWS + (b + 1) * ROWS] for h in (0, 1)],
                axis=0,
            )
            for b in range(ny)
        ]

    def natural(x):
        return jnp.concatenate(
            [x[(2 * b + h) * ROWS : (2 * b + h + 1) * ROWS] for h in (0, 1) for b in range(ny)],
            axis=0,
        )

    loads[1].wait()
    slot = fetch[0, 0]
    held = stash[slot]
    for b, rows in enumerate(permuted(held[:, W_IN:].astype(F32))):
        reto[b] = rows.astype(BF16)
    retq[...] = held[:, :W_IN]

    def across_core(src, via):
        return sends(src, other_core).send(src, via, other_core)

    def to_mirror(via, dst):
        return sends(via, next_chip).send(via, dst, next_chip)

    core_o = across_core(reto, reto_via)
    core_q = across_core(retq, retq_via)

    loads[2].wait()
    core_p = across_core(attn_in, evp_via)
    loads[3].wait()
    row_id = lax.broadcasted_iota(jnp.int32, (tok, tok), 0)
    col_id = lax.broadcasted_iota(jnp.int32, (tok, tok), 1)
    seg_cols = jnp.broadcast_to(seg[...].astype(F32), (tok, tok))
    allowed = (seg_cols == jnp.transpose(seg_cols)) & (col_id <= row_id)
    q = stack_heads(attn_in[:, :QW], heads)
    k = attn_in[:, QW : QW + HEAD]
    v = attn_in[:, QW + HEAD : W_IN]
    weights = probabilities(q, k, allowed, heads).astype(BF16)
    att = unstack_heads(dot(weights, v), heads)
    attb[...] = att.astype(BF16)
    core_a = across_core(attb, eva_via)
    for b, rows in enumerate(permuted(att)):
        A[0, b] = rows.astype(BF16)


    def two_way(parts):
        return [
            (way, p, 4 if (p < parts // 2) == (way == 1) else 3)
            for p in range(parts)
            for way in (1, -1)
        ]

    def a_piece(rel, h):
        return A.at[NEAR.index(rel), pl.ds(h * ny // A_PARTS, ny // A_PARTS)]

    def ring_rel(rel):
        return 4 if rel == -4 else rel

    gather_a = Gather(
        sends(A.at[pl.ds(0, nz - 1)], some_z),
        nz,
        z,
        zdev,
        two_way(A_PARTS),
        lambda way, h, r: a_piece(ring_rel(-way * r), h),
        lambda way, h, r: a_piece(ring_rel(-way * (r + 1)), h),
    )

    def o_piece(way, h, r):
        return O.at[at_z(-way * r), pl.ds(h * ny // O_PARTS, ny // O_PARTS)]

    gather_o = Gather(
        sends(O.at[pl.ds(0, nz - 1)], some_z), nz, z, zdev, two_way(O_PARTS), o_piece, o_piece
    )

    sub = nz * ROWS // G_PARTS

    def g_piece(way, h, r):
        return G.at[at_y(-way * r), xh, pl.ds(h * sub, sub)]

    gather_g = Gather(
        sends(G.at[pl.ds(0, ny - 1), 0], some_y), ny, y, ydev, two_way(G_PARTS), g_piece, g_piece
    )

    def other_piece(way, h, r):
        return G.at[at_y(-way * r), 1 - xh]

    gather_other = Gather(
        sends(G.at[pl.ds(0, 2 * X_HOPS), 0], some_y),
        ny,
        y,
        ydev,
        ((1, 0, X_HOPS), (-1, 0, X_HOPS)),
        other_piece,
        other_piece,
    )
    across = [0] + [rel for rel in NEAR if abs(rel) > X_HOPS]
    g_x = sends(G.at[pl.ds(0, len(across)), 0], xpeer)
    g_x_moves = {}

    def send_across(rel):
        ref = G.at[at_y(rel), xh]
        g_x_moves[rel] = g_x.send(ref, ref, xpeer)

    gather_a.step(0)

    def cotangent_piece(group, recv, h, at):
        group.whole(recv).wait_recv()
        for p in range(nz // 2):
            rows = [to_wide(b1r[h * nz + 2 * p + j].astype(F32)) for j in (0, 1)]
            G[y, at, pl.ds(2 * ROWS * p, 2 * ROWS), :] = jnp.concatenate(rows, axis=0).astype(BF16)

    cotangent_piece(b1, b1_recv, 0, xh)
    gather_g.step(0)
    send_across(0)
    gather_a.step(1)

    for load in loads[4:]:
        load.wait()

    Z_SPLIT = ((0, 5, 3), (5, 3, 2))
    z_sums = []
    for lo, count, cut in Z_SPLIT:
        z_sums.append(
            RingSum(
                sends(O.at[pl.ds(0, nz - 1), pl.ds(0, count)], some_z),
                z,
                nz,
                zdev,
                lambda side, r, lo=lo, count=count: zslots.at[side, r, pl.ds(lo, count)],
                ((0, cut), (cut, count - cut)),
            )
        )

    def head_grad_part(rels):
        for rel in rels:
            b = at_y(rel)
            res = dot(G[b].reshape(2 * nz * ROWS, C), weight[...], 1, 1)
            for d in range(nz):
                both = [res[(h * nz + d) * ROWS : (h * nz + d + 1) * ROWS] for h in (0, 1)]
                part[d, NEAR.index(rel)] = jnp.concatenate(both, axis=0).astype(BF16)

    def head_grad_step(i, r):
        lo, count, _ = Z_SPLIT[i]
        z_sums[i].step(r, lambda rel: part[at_z(rel), pl.ds(lo, count)].astype(F32))

    RUNS = nz // 2
    y_sums = [
        RingSum(
            sends(G.at[pl.ds(0, ny - 1), 0], some_y),
            y,
            ny,
            ydev,
            lambda side, r, g=g: yslots.at[g, side, r],
            ((0, RUNS * ROWS), (RUNS * ROWS, RUNS * ROWS)),
        )
        for g in (0, 1)
    ]

    def branch_term(g, rel):
        rows = A[pl.ds(g * RUNS, RUNS), at_y(rel)].reshape(RUNS * 2 * ROWS, QW)
        return dot(rows, weight[...])

    def branch_step(g, r):
        y_sums[g].step(r, lambda rel: branch_term(g, rel))

    f5 = sends(f5r.at[pl.ds(0, nz - 1)], some_z)
    f5_recv = pool.new()
    keep, x_moves = {}, {}

    def branch_x(g):
        total = branch_term(g, 0) + y_sums[g].last()
        halves = [
            jnp.concatenate(
                [total[(2 * j + h) * ROWS : (2 * j + h + 1) * ROWS] for j in range(RUNS)], axis=0
            )
            for h in (0, 1)
        ]
        xs[g] = jnp.where(xh == 0, halves[1], halves[0]).astype(BF16)
        x_moves[g] = sends(xs.at[g], xpeer).send(xs.at[g], xr.at[g], xpeer)
        keep[g] = jnp.where(xh == 0, halves[0], halves[1])

    def branch_end(g):
        x_moves[g].wait_recv()
        total = keep[g] + xr[g].astype(F32)
        for j in reversed(range(RUNS)):
            slot = g * RUNS + j
            rel = NEAR[slot]
            tall = to_tall(total[j * ROWS : (j + 1) * ROWS]).astype(BF16)
            if rel == 0:
                f5r[z] = tall
            else:
                f5s[slot] = tall
                f5.send(f5s.at[slot], f5r.at[z], zdev(at_z(rel)), f5_recv)

    def weight_grad_part(i):
        cols = pl.ds(i * (C // 4), C // 4)
        wgrad_out[:, cols] = dot(
            OT[...], G[:, :, :, cols].reshape(nt * nz * ROWS, C // 4)
        ).astype(BF16)

    def arrange_outputs():
        for b in range(ny):
            x = O[:, b].astype(F32)
            rows = [x[d, h * ROWS : (h + 1) * ROWS] for h in (0, 1) for d in range(nz)]
            block = jnp.concatenate(rows, axis=0)
            width = 2 * nz * ROWS
            OT[:, b * width : (b + 1) * width] = jnp.transpose(block).astype(BF16)

    core_o.wait_recv()
    move_ret_o = to_mirror(reto_via, O.at[z])
    gather_g.step(1)
    g_x_moves[0].wait_recv()
    gather_other.step(0)
    gather_a.step(2)
    head_grad_part((0,))
    branch_step(0, 0)
    gather_g.step(2)
    gather_other.step(1)
    gather_a.step(3)
    head_grad_part((1, -1))
    move_ret_o.wait_recv()
    gather_o.step(0)
    branch_step(0, 1)
    gather_g.step(3)
    send_across(3)
    send_across(-3)
    gather_other.step(2)
    head_grad_part((2, -2))
    head_grad_step(0, 0)
    gather_a.step(4)
    branch_step(1, 0)
    branch_step(0, 2)
    gather_g.step(4)
    send_across(4)
    gather_o.step(1)
    head_grad_step(0, 1)
    branch_step(1, 1)
    g_x_moves[3].wait_recv()
    g_x_moves[-3].wait_recv()
    head_grad_part((3, -3))
    branch_step(0, 3)
    g_x_moves[4].wait_recv()
    head_grad_part((4,))
    head_grad_step(1, 0)
    core_q.wait_recv()
    move_ret_q = to_mirror(retq_via, retr)
    gather_o.step(2)
    head_grad_step(0, 2)
    branch_step(1, 2)
    head_grad_step(1, 1)
    core_p.wait_recv()
    core_a.wait_recv()
    move_ev_p = to_mirror(evp_via, evp)
    move_ev_a = to_mirror(eva_via, eva)
    branch_x(0)
    gather_o.step(3)
    head_grad_step(0, 3)
    branch_step(1, 3)
    head_grad_step(1, 2)
    branch_end(0)
    gather_o.step(4)
    arrange_outputs()
    for i in range(2):
        weight_grad_part(i)
    head_grad_step(1, 3)
    branch_x(1)
    for i in range(2, 4):
        weight_grad_part(i)

    move_ret_q.wait_recv()
    end = jnp.int32(0)
    seg_row = jnp.zeros((tok, tok), jnp.int32)
    seg_col = jnp.zeros((tok, tok), jnp.int32)
    for c in range(lens.shape[1]):
        end = end + lens[0, c]
        seg_row += (row_id >= end).astype(jnp.int32)
        seg_col += (col_id >= end).astype(jnp.int32)
    allowed = (seg_row == seg_col) & (col_id <= row_id)
    q = stack_heads(retr[:, :QW], heads)
    k = retr[:, QW : QW + HEAD]
    v = retr[:, QW + HEAD : W_IN]
    probs = probabilities(q, k, allowed, heads)
    old = natural(O[z].astype(F32).reshape(tok, QW))

    branch_end(1)

    sums = jnp.concatenate([z_sums[0].last(), z_sums[1].last()], axis=0)
    total = part[z].astype(F32) + sums
    for j, rel in enumerate(NEAR):
        for h in (0, 1):
            row = pl.multiple_of((h * ny + at_y(rel)) * ROWS, ROWS)
            dnat[pl.ds(row, ROWS), :] = total[j, h * ROWS : (h + 1) * ROWS]
    d_out = dnat[...].astype(BF16)
    d_heads = stack_heads(d_out, heads)
    grad_v = dot(probs.astype(BF16), d_heads, 0, 0)
    grad_p = dot(d_heads, v, 1, 1)
    inner = jnp.sum(d_heads.astype(F32) * stack_heads(old, heads), axis=-1, keepdims=True)
    grad_s = (probs * (grad_p - inner)).astype(BF16)
    grad_k = dot(grad_s, q, 0, 0) * HEAD ** (-0.5)
    shs[:, :HEAD] = grad_k.astype(BF16)
    shs[:, HEAD:] = grad_v.astype(BF16)
    move_shared = sends(shs, pair).send(shs, shr, pair)
    grad_q = dot(grad_s, k) * HEAD ** (-0.5)
    agrad_out[:, :QW] = unstack_heads(grad_q, heads).astype(BF16)
    move_ev_p.wait_recv()
    move_ev_a.wait_recv()
    for i in range(stash.shape[0]):
        here = evict[0] == i
        stash_out[i, :, :W_IN] = jnp.where(here, evp[...], stash[i, :, :W_IN])
        stash_out[i, :, W_IN:] = jnp.where(here, eva[...], stash[i, :, W_IN:])

    move_shared.wait_recv()
    agrad_out[:, QW:] = (shs[...].astype(F32) + shr[...].astype(F32)).astype(BF16)

    f5.whole(f5_recv).wait_recv()
    for d in range(nz):
        cols = slice(d * C, (d + 1) * C)
        summed = to_wide(f5r[d].astype(F32))
        lay_out[:, cols] = (resid[:, cols].astype(F32) + summed).astype(BF16)

    for group in groups:
        group.finish()


def body(
    dims,
    resid_in,
    attn_in,
    seg_fwd,
    out_weight,
    stash_held,
    len_bwd,
    out_grad,
    evict_slot,
    fetch_slot,
):
    n_sec, nz, nt = dims
    ny = nt // 2
    tok = nt * ROWS
    QW, C = out_weight.shape[1:]
    D = resid_in.shape[-1]
    W_IN = QW + 2 * HEAD
    slots, width = stash_held.shape[1], stash_held.shape[-1]
    vmem, smem, hbm = (
        pl.BlockSpec(memory_space=s) for s in (pltpu.VMEM, pltpu.SMEM, pltpu.HBM)
    )

    def buf(*shape):
        return pltpu.VMEM(shape, BF16)

    outs = pl.pallas_call(
        functools.partial(kernel, dims),
        out_shape=(
            jax.ShapeDtypeStruct((ROWS, D), BF16),
            jax.ShapeDtypeStruct((slots, tok, width), BF16),
            jax.ShapeDtypeStruct((QW, C), BF16),
            jax.ShapeDtypeStruct((tok, W_IN), BF16),
        ),
        in_specs=[hbm] * 7 + [smem] * 2,
        out_specs=(vmem,) * 4,
        scratch_shapes=[
            buf(ROWS, D),
            buf(tok, W_IN),
            pltpu.VMEM((1, tok), jnp.int32),
            pltpu.SMEM(len_bwd.shape[1:], jnp.int32),
            buf(QW, C),
            buf(slots, tok, width),
            buf(ROWS, D),
            buf(nz, 2 * ROWS, C // 2),
            buf(2 * nz, 2 * ROWS, C // 2),
            buf(ny, 2, nz * ROWS, C),
            buf(nz, ny, 2 * ROWS, QW),
            buf(2, nz // 2 + 1, ny, 2 * ROWS, QW),
            buf(nz, ny, 2 * ROWS, QW),
            buf(nz, ny, 2 * ROWS, QW),
            buf(2, 2, ny // 2 + 1, nz * ROWS, C),
            buf(nz, 2 * ROWS, C // 2),
            buf(nz, 2 * ROWS, C // 2),
            buf(2, nz // 2 * ROWS, C),
            buf(2, nz // 2 * ROWS, C),
            buf(tok, QW),
            buf(ny, 2 * ROWS, QW),
            buf(ny, 2 * ROWS, QW),
            buf(tok, W_IN),
            buf(tok, W_IN),
            buf(tok, W_IN),
            buf(tok, W_IN),
            buf(tok, W_IN),
            buf(tok, QW),
            buf(tok, QW),
            buf(tok, 2 * HEAD),
            buf(tok, 2 * HEAD),
            buf(QW, nt * nz * ROWS),
            pltpu.VMEM((tok, QW), F32),
            pltpu.SemaphoreType.DMA((SEMS,)),
            pltpu.SemaphoreType.DMA((7,)),
        ],
        compiler_params=pltpu.CompilerParams(
            collective_id=0, has_side_effects=True, vmem_limit_bytes=48 * 2**20
        ),
    )(
        *(
            pltpu.with_memory_space_constraint(x, pltpu.HBM) if x.size > 1 else x
            for x in (
                resid_in[0],
                attn_in[0],
                seg_fwd[0],
                len_bwd[0],
                out_weight[0],
                stash_held[0],
                out_grad[0],
                evict_slot,
                fetch_slot,
            )
        )
    )
    return tuple(x[None] for x in outs)


def solution(mesh):
    dims = tuple(mesh.shape[a] for a in ("section", "dp", "tensor"))
    placed = (
        P("section", ("dp", "tensor"), None),
        P("section", "dp", "tensor"),
        P("section", "dp", None),
        P("section", "tensor", "dp"),
        P("section", None, "dp", "tensor"),
        P("section", "dp", None),
        P("section", ("dp", "tensor"), None),
        P("section"),
        P("section", "dp"),
    )
    return jax.shard_map(
        functools.partial(body, dims),
        mesh=mesh,
        in_specs=placed,
        out_specs=(
            P("section", ("dp", "tensor"), None),
            P("section", None, "dp", "tensor"),
            P("section", "tensor", "dp"),
            P("section", "dp", "tensor"),
        ),
        check_vma=False,
    )
```

time: 92.4 us -> 76.9 us (0.83)
  the two profiles are of different devices: /device:TPU:20 before, /device:TPU:8 now
where the time goes in v2:
time: 76.9 us; the launch traced here: 76.8 us
  Pallas kernels  71.6 us (93%)
  local copies, waits for them, and re-layouts  3.25 us (4%)
  between operations  1.93 us (3%)
    pallas_call x1, Pallas kernels, body(): pl.pallas_call(functools.partial(kernel, dims), out_shape=(jax.ShapeDtype...  71.6 us
    unnamed x4, local copies, waits for them, and re-layouts  3.25 us

profile of v2, /device:TPU:8, one launch (start us, length us, event | category | flops | bytes accessed | tf_op | source)
XLA Modules:
  0.0 76.8 jit_solution(34951222986425206)
XLA Ops:
  1.9 71.6 %shard_map.120 = (bf16[8,8192]{1,0:T(8,128)(2,1)S(1)}, bf16[3,128,1280]{2,1,0:T(8,128)(2,1)S(1)}, bf16[512,1024]{1,0:T(8,128)(2,1)S(1)}, bf16[128,768]{1,0:T(8,128)(2,1)S(1)}) custom-call(bf16[8,8192]{1,0:T(8,128)(2,1)} %bitcast.18, bf16[128,768]{1,0:T(8,128)(2,1)} %bitcast.17, s32[1,128]{1,0:T(1,128)} %bitcast.20, s32[1,8]{1,0:T(1,128)} %bitcast.21, ...), custom_call_target="tpu_custom_call" | custom-call | tf_op jit(solution)/shard_map/pallas_call | solution.py:632
  73.5 0.7 copy.19
  74.2 0.9 %copy.20 = bf16[1,3,128,1280]{3,2,1,0:T(8,128)(2,1)} copy(bf16[1,3,128,1280]{3,2,1,0:T(8,128)(2,1)S(1)} %bitcast.12) | data formatting | bytes 1966080
  75.1 1.0 %copy.21 = bf16[1,512,1024]{2,1,0:T(8,128)(2,1)} copy(bf16[1,512,1024]{2,1,0:T(8,128)(2,1)S(1)} %bitcast.11) | data formatting | bytes 2097152
  76.1 0.7 copy.22

commit v3 on v2

--- a/solution.py
+++ b/solution.py
@@ -146,7 +146,7 @@
 NEAR = (0, 1, -1, 2, -2, 3, -3, 4)
 FAR = (4, 3, -3, 2, -2, 1, -1, 0)
 A_PARTS, O_PARTS, G_PARTS = 2, 2, 4
-X_HOPS = 2
+X_HOPS = 1
 
 
 def kernel(
@@ -487,25 +487,28 @@
             width = 2 * nz * ROWS
             OT[:, b * width : (b + 1) * width] = jnp.transpose(block).astype(BF16)
 
-    core_o.wait_recv()
-    move_ret_o = to_mirror(reto_via, O.at[z])
     gather_g.step(1)
     g_x_moves[0].wait_recv()
     gather_other.step(0)
+    core_o.wait_recv()
+    move_ret_o = to_mirror(reto_via, O.at[z])
     gather_a.step(2)
     head_grad_part((0,))
     branch_step(0, 0)
     gather_g.step(2)
+    send_across(2)
+    send_across(-2)
     gather_other.step(1)
     gather_a.step(3)
     head_grad_part((1, -1))
-    move_ret_o.wait_recv()
-    gather_o.step(0)
     branch_step(0, 1)
     gather_g.step(3)
     send_across(3)
     send_across(-3)
-    gather_other.step(2)
+    move_ret_o.wait_recv()
+    gather_o.step(0)
+    g_x_moves[2].wait_recv()
+    g_x_moves[-2].wait_recv()
     head_grad_part((2, -2))
     head_grad_step(0, 0)
     gather_a.step(4)
@@ -541,12 +544,8 @@
     branch_end(0)
     gather_o.step(4)
     arrange_outputs()
-    for i in range(2):
-        weight_grad_part(i)
     head_grad_step(1, 3)
     branch_x(1)
-    for i in range(2, 4):
-        weight_grad_part(i)
 
     move_ret_q.wait_recv()
     end = jnp.int32(0)
@@ -583,6 +582,8 @@
     move_shared = sends(shs, pair).send(shs, shr, pair)
     grad_q = dot(grad_s, k) * HEAD ** (-0.5)
     agrad_out[:, :QW] = unstack_heads(grad_q, heads).astype(BF16)
+    for i in range(4):
+        weight_grad_part(i)
     move_ev_p.wait_recv()
     move_ev_a.wait_recv()
     for i in range(stash.shape[0]):

time: 76.9 us -> 74.1 us (0.964)
  Pallas kernels: 71.6 us -> 68.8 us
    pallas_call x1, Pallas kernels: 71.6 us -> 68.8 us  [body(): pl.pallas_call(functools.partial(kernel, dims), out_shape=(jax.ShapeDtype...]
where the time goes in v3:
time: 74.1 us; the launch traced here: 74 us
  Pallas kernels  68.8 us (93%)
  local copies, waits for them, and re-layouts  3.25 us (4%)
  between operations  1.93 us (3%)
    pallas_call x1, Pallas kernels, body(): pl.pallas_call(functools.partial(kernel, dims), out_shape=(jax.ShapeDtype...  68.8 us
    unnamed x4, local copies, waits for them, and re-layouts  3.25 us

profile of v3, /device:TPU:8, one launch (start us, length us, event | category | flops | bytes accessed | tf_op | source)
XLA Modules:
  0.0 74.0 jit_solution(539161230373442739)
XLA Ops:
  1.9 68.8 %shard_map.120 = (bf16[8,8192]{1,0:T(8,128)(2,1)S(1)}, bf16[3,128,1280]{2,1,0:T(8,128)(2,1)S(1)}, bf16[512,1024]{1,0:T(8,128)(2,1)S(1)}, bf16[128,768]{1,0:T(8,128)(2,1)S(1)}) custom-call(bf16[8,8192]{1,0:T(8,128)(2,1)} %bitcast.18, bf16[128,768]{1,0:T(8,128)(2,1)} %bitcast.17, s32[1,128]{1,0:T(1,128)} %bitcast.20, s32[1,8]{1,0:T(1,128)} %bitcast.21, ...), custom_call_target="tpu_custom_call" | custom-call | tf_op jit(solution)/shard_map/pallas_call | solution.py:633
  70.7 0.7 copy.19
  71.4 0.9 %copy.20 = bf16[1,3,128,1280]{3,2,1,0:T(8,128)(2,1)} copy(bf16[1,3,128,1280]{3,2,1,0:T(8,128)(2,1)S(1)} %bitcast.12) | data formatting | bytes 1966080
  72.3 1.0 %copy.21 = bf16[1,512,1024]{2,1,0:T(8,128)(2,1)} copy(bf16[1,512,1024]{2,1,0:T(8,128)(2,1)S(1)} %bitcast.11) | data formatting | bytes 2097152
  73.3 0.7 copy.22

commit v4 on v3

--- a/solution.py
+++ b/solution.py
@@ -542,8 +542,6 @@
     branch_step(1, 3)
     head_grad_step(1, 2)
     branch_end(0)
-    gather_o.step(4)
-    arrange_outputs()
     head_grad_step(1, 3)
     branch_x(1)
 
@@ -582,6 +580,8 @@
     move_shared = sends(shs, pair).send(shs, shr, pair)
     grad_q = dot(grad_s, k) * HEAD ** (-0.5)
     agrad_out[:, :QW] = unstack_heads(grad_q, heads).astype(BF16)
+    gather_o.step(4)
+    arrange_outputs()
     for i in range(4):
         weight_grad_part(i)
     move_ev_p.wait_recv()

time: 74.1 us -> 74.1 us (level)
  the two profiles are of different devices: /device:TPU:8 before, /device:TPU:24 now
where the time goes in v4:
time: 74.1 us; the launch traced here: 73.9 us
  Pallas kernels  68.8 us (93%)
  local copies, waits for them, and re-layouts  3.25 us (4%)
  between operations  1.93 us (3%)
    pallas_call x1, Pallas kernels, body(): pl.pallas_call(functools.partial(kernel, dims), out_shape=(jax.ShapeDtype...  68.8 us
    unnamed x4, local copies, waits for them, and re-layouts  3.25 us

profile of v4, /device:TPU:24, one launch (start us, length us, event | category | flops | bytes accessed | tf_op | source)
XLA Modules:
  0.0 73.9 jit_solution(2782778729721195571)
XLA Ops:
  1.9 68.8 %shard_map.120 = (bf16[8,8192]{1,0:T(8,128)(2,1)S(1)}, bf16[3,128,1280]{2,1,0:T(8,128)(2,1)S(1)}, bf16[512,1024]{1,0:T(8,128)(2,1)S(1)}, bf16[128,768]{1,0:T(8,128)(2,1)S(1)}) custom-call(bf16[8,8192]{1,0:T(8,128)(2,1)} %bitcast.18, bf16[128,768]{1,0:T(8,128)(2,1)} %bitcast.17, s32[1,128]{1,0:T(1,128)} %bitcast.20, s32[1,8]{1,0:T(1,128)} %bitcast.21, ...), custom_call_target="tpu_custom_call" | custom-call | tf_op jit(solution)/shard_map/pallas_call | solution.py:633
  70.7 0.7 copy.19
  71.3 0.9 %copy.20 = bf16[1,3,128,1280]{3,2,1,0:T(8,128)(2,1)} copy(bf16[1,3,128,1280]{3,2,1,0:T(8,128)(2,1)S(1)} %bitcast.12) | data formatting | bytes 1966080
  72.3 1.0 %copy.21 = bf16[1,512,1024]{2,1,0:T(8,128)(2,1)} copy(bf16[1,512,1024]{2,1,0:T(8,128)(2,1)S(1)} %bitcast.11) | data formatting | bytes 2097152
  73.3 0.7 copy.22
